TPU v7x, 256 devices: a whole 4x4x8 slice. The times are simulated.
256 devices in a mesh: wide: 32 (over x_lo, z, core), narrow: 8 (over x_hi, y).
Axes of the slice: x: 4 (x_hi: 2, x_lo: 2; x = x_hi * 2 + x_lo), y: 4, z: 8, core: 2. Of those that a mesh axis runs over, the one named last changes fastest.
Arguments:
- activations: float32 [1024, 17408], P('wide', 'narrow'), may hold values from -6 to 6
- act_basis: float32 [17408, 17408], P('narrow', 'wide'), may hold values from -0.046875 to 0.046875
- grads: float32 [1024, 5120], P(None, 'wide'), may hold values from -0.3 to 0.3
- grad_basis: float32 [5120, 5120], P('wide', 'narrow'), may hold values from -0.078125 to 0.078125
- seq_ids: int32 [1024], replicated, may hold values from 0 to 3, never falling along the last dimension, each value on 1 to 512 neighbouring positions
Outputs:
- eigenvalues: float32 [17408, 5120], P('wide', 'narrow')
Inputs may be any that keep to these rules, and one draw needn't show every extreme that they name: `seq_ids`: never falling along the rows; every sequence has at least one row and at most 512 rows, and one sequence has exactly 512.
All inputs are finite; a program needn't handle non-finite values.
Results may differ from a plain program's by a relative error of at most 0.0003.
Values sent between devices are 32-bit elements; how exact they have to be, the bound alone decides.
No kernel may reach another device: no remote copies, remote signals or barrier semaphores. Data moves between devices by JAX's collectives and lax.ppermute only.
A program may use at most 64 MiB of HBM per device.

v0:
```python
import jax
import jax.numpy as jnp
from jax import lax
from jax.sharding import Mesh
from jax.sharding import PartitionSpec as P

SEQS = 4
SEQ_MOST = 512
WIDE = ("wide_0", "wide_1", "wide_2")


def filled_up(lines, devices):
    spare = -len(lines) % devices
    return jnp.pad(lines, [(0, spare)] + [(0, 0)] * (lines.ndim - 1))


def from_everyone(value, axis):
    devices = lax.axis_size(axis)
    return lax.all_to_all(
        jnp.broadcast_to(value[None], (devices, *value.shape)), axis, 0, 0, tiled=True
    )


def in_order(blocks, dim):
    blocks = jnp.moveaxis(blocks, 0, dim)
    dims = blocks.shape
    return blocks.reshape(*dims[:dim], dims[dim] * dims[dim + 1], *dims[dim + 2 :])


def gather_axes(value, axes, dim):
    far, near = axes
    first = from_everyone(value, far)
    blocks = jnp.swapaxes(from_everyone(first, near), 0, 1)
    return in_order(blocks.reshape(-1, *value.shape), dim)


def in_blocks(value, dim, devices):
    dims = value.shape
    blocks = value.reshape(*dims[:dim], devices, dims[dim] // devices, *dims[dim + 1 :])
    return jnp.moveaxis(blocks, dim, 0)


def sent_and_summed(value, axis, dim):
    blocks = in_blocks(value, dim, lax.axis_size(axis))
    arrived = lax.all_to_all(blocks, axis, split_axis=0, concat_axis=0, tiled=True)
    return arrived.sum(axis=0)


def summed_rows(value, axes, dim):
    far, near = axes
    blocks = in_blocks(value, dim, lax.axis_size(far))
    nearer = sent_and_summed(blocks, near, dim + 1)
    arrived = lax.all_to_all(nearer, far, split_axis=0, concat_axis=0, tiled=True)
    return arrived.sum(axis=0)


def nested_sum(value, axes):
    lines = value.reshape(-1, value.shape[-1])
    padded = filled_up(lines, lax.axis_size(axes[0]) * lax.axis_size(axes[1]))
    whole = gather_axes(summed_rows(padded, axes, 0), axes, 0)
    return lax.slice_in_dim(whole, 0, len(lines)).reshape(value.shape)


def seq_window(rotated_acts, rotated_grads, seq_ids, seq_label):
    token_rows = rotated_grads.shape[0]
    first_row = jnp.sum((seq_ids < seq_label).astype(jnp.int32))
    window_start = jnp.minimum(first_row, token_rows - SEQ_MOST)
    acts_window = lax.dynamic_slice_in_dim(rotated_acts, window_start, SEQ_MOST, 0)
    grads_window = lax.dynamic_slice_in_dim(rotated_grads, window_start, SEQ_MOST, 0)
    ids_window = lax.dynamic_slice_in_dim(seq_ids, window_start, SEQ_MOST, 0)
    seq_mask = (ids_window == seq_label).astype(jnp.float32)[:, None]
    return (acts_window, grads_window * seq_mask)


def per_device(activations, act_basis, grads, grad_basis, seq_ids):
    highest = lax.Precision.HIGHEST
    gathered = lax.all_gather(activations, WIDE, axis=0, tiled=True)
    partial_acts = jnp.dot(
        gathered, act_basis, precision=highest, preferred_element_type=jnp.float32
    )
    rotated_acts = lax.psum(partial_acts, "narrow")
    partial_grads = jnp.dot(
        grads, grad_basis, precision=highest, preferred_element_type=jnp.float32
    )
    rotated_grads = nested_sum(partial_grads, (("wide_0", "wide_1"), "wide_2"))
    out_cols = rotated_grads.shape[1]
    running = jnp.zeros((rotated_acts.shape[1], out_cols), jnp.float32)
    for seq_label in range(SEQS):
        acts_window, grads_window = seq_window(rotated_acts, rotated_grads, seq_ids, seq_label)
        moment = jnp.dot(
            acts_window.T, grads_window, precision=highest, preferred_element_type=jnp.float32
        )
        running = running + moment * moment
    return running / jnp.float32(SEQS)


def solution(mesh):
    split = Mesh(
        mesh.devices.reshape(2, 8, 2, mesh.shape["narrow"]),
        ("wide_0", "wide_1", "wide_2", "narrow"),
    )
    return jax.shard_map(
        per_device,
        mesh=split,
        in_specs=(P(WIDE, "narrow"), P("narrow", WIDE), P(None, WIDE), P(WIDE, "narrow"), P()),
        out_specs=P(WIDE, "narrow"),
        check_vma=False,
    )
```

profile of v0, /device:TPU:32, one launch (start us, length us, event | category | flops | bytes accessed | tf_op | source)
XLA Modules:
  0.0 276.0 jit_solution(7294936986308628746)
XLA Ops:
  6.5 0.0 copy-start
  6.5 0.0 all-gather.2.cloned.1.call-start
  6.5 0.7 all-gather.2.cloned.1.call-update
  7.3 0.4 copy-done
  7.6 3.9 %fusion.29 = f32[1024,640]{1,0:T(8,128)S(1)} fusion(f32[1024,160]{0,1:T(8,128)S(1)} %copy-done, f32[160,640]{1,0:T(8,128)} %param.8), kind=kOutput, calls=%fused_computation.42 | convolution fusion | flops 1258291200 | bytes 3686400 | tf_op jit(solution)/shard_map/dot_general | solution.py:82
  11.6 0.2 copy.11
  11.8 5.8 %all_to_all.20 = f32[2,16,32,640]{3,2,1,0:T(8,128)S(1)} all-to-all(f32[2,16,32,640]{3,2,1,0:T(8,128)S(1)} %bitcast.15), channel_id=1, replica_groups=mesh['wide_0'=2,'wide_1'=8,'wide_2'=2,'narrow'=8] {'wide_2'}, dimensions={0} | all-to-all | bytes 5242880 | tf_op jit(solution)/shard_map/all_to_all | solution.py:45
  17.6 1.3 reduce_sum.55
  18.9 54.5 %all_to_all.21 = f32[16,32,640]{2,1,0:T(8,128)S(1)} all-to-all(f32[16,32,640]{2,1,0:T(8,128)} %reduce_sum.55), channel_id=1, replica_groups=mesh['wide_0'=2,'wide_1'=8,'wide_2'=2,'narrow'=8] {'wide_0','wide_1'}, dimensions={0} | all-to-all | bytes 2621440 | tf_op jit(solution)/shard_map/all_to_all | solution.py:53
  73.5 0.1 reduce_sum.56
  73.5 1.2 broadcast_in_dim.4
  74.7 6.4 %all-to-all-start.2 = ((f32[16,32,640]{2,1,0:T(8,128)}), f32[16,32,640]{2,1,0:T(8,128)S(1)}, u32[]{:S(2)}, u32[]{:S(2)}) async-start(f32[16,32,640]{2,1,0:T(8,128)} %broadcast_in_dim.4), calls=%async_computation.2 | async-start | bytes 2621440 | tf_op jit(solution)/shard_map/all_to_all | solution.py:19
  81.2 0.0 all-reduce.2.cloned.1.call-start
  81.2 52.6 %all-gather.2.cloned.1.call-done = f32[1024,2176]{1,0:T(8,128)} async-done(((f32[32,2176]{1,0:T(8,128)}), f32[1024,2176]{1,0:T(8,128)}) %all-gather.2.cloned.1.call-update) | async-done | bytes 8912912 | tf_op jit(solution)/shard_map/all_gather | solution.py:77
  133.8 21.9 %fusion.28 = f32[1024,544]{0,1:T(8,128)} fusion(f32[1024,2176]{1,0:T(8,128)} %all-gather.2.cloned.1.call-done, f32[2176,544]{0,1:T(8,128)} %param.6), kind=kOutput, calls=%fused_computation.41 | convolution fusion | flops 14545846272 | bytes 15876096 | tf_op jit(solution)/shard_map/dot_general | solution.py:78
  155.7 0.0 copy-start.2
  155.7 0.0 all-reduce.2.cloned.1.call-update
  155.7 0.7 copy-done.2
  156.4 0.7 convert_reduce_fusion
  159.8 0.1 fusion.27
  159.9 0.0 all-to-all-done.2
  159.9 0.3 broadcast_in_dim.5
  160.2 5.8 %all_to_all.22 = f32[2,16,32,640]{3,2,1,0:T(8,128)S(1)} all-to-all(f32[2,16,32,640]{3,2,1,0:T(8,128)S(1)} %broadcast_in_dim.5), channel_id=1, replica_groups=mesh['wide_0'=2,'wide_1'=8,'wide_2'=2,'narrow'=8] {'wide_2'}, dimensions={0} | all-to-all | bytes 5242880 | tf_op jit(solution)/shard_map/all_to_all | solution.py:19
  166.0 0.2 copy.9
  166.2 87.8 %all-reduce.2.cloned.1.call-done = f32[1024,544]{0,1:T(8,128)} async-done(((f32[1024,544]{0,1:T(8,128)}), f32[1024,544]{0,1:T(8,128)}) %all-reduce.2.cloned.1.call-update) | async-done | bytes 2228240 | tf_op jit(solution)/shard_map/psum | solution.py:81
  254.0 0.0 copy-start.1
  254.0 4.5 %convolution_multiply_fusion.1 = f32[544,640]{1,0:T(8,128)S(1)} fusion(f32[1024,640]{1,0:T(8,128)S(1)} %bitcast.11, s32[]{:T(128)S(6)} %select_n.10, f32[1024,544]{0,1:T(8,128)} %all-reduce.2.cloned.1.call-done, f32[512]{0:T(512)S(1)} %get-tuple-element.10), kind=kOutput, calls=%fused_computation.2 | convolution fusion | flops 2139770880 | bytes 3820544 | tf_op jit(solution)/shard_map/dot_general | solution.py:90
  258.5 0.0 copy-done.1
  258.5 3.1 %convolution_multiply_fusion.2 = f32[544,640]{1,0:T(8,128)S(1)} fusion(f32[1024,640]{1,0:T(8,128)S(1)} %bitcast.12, s32[]{:T(128)S(6)} %select_n.9, f32[1024,544]{0,1:T(8,128)S(1)} %copy-done.1, f32[512]{0:T(512)S(1)} %get-tuple-element.12), kind=kOutput, calls=%fused_computation.3 | convolution fusion | flops 2139770880 | bytes 3820544 | tf_op jit(solution)/shard_map/dot_general | solution.py:90
  261.7 3.2 %fusion.1 = f32[544,640]{1,0:T(8,128)S(1)} fusion(f32[544,640]{1,0:T(8,128)S(1)} %convolution_multiply_fusion.1, f32[544,640]{1,0:T(8,128)S(1)} %convolution_multiply_fusion.2, f32[1024,640]{1,0:T(8,128)S(1)} %bitcast.13, s32[]{:T(128)S(6)} %select_n.8, f32[1024,544]{0,1:T(8,128)S(1)} %copy-done.1, f32[512]{0:T(512)S(1)} %get-tuple-element.11), kind=kOutput, calls=%fused_computation.6 | convolution fusion | flops 2140467200 | bytes 6605824 | tf_op jit(solution)/shard_map/dot_general | solution.py:90
  264.9 4.2 %fusion.3 = f32[544,640]{1,0:T(8,128)} fusion(f32[544,640]{1,0:T(8,128)S(1)} %fusion.1, f32[1024,640]{1,0:T(8,128)S(1)} %bitcast.14, s32[]{:T(128)S(6)} %select_n.11, f32[1024,544]{0,1:T(8,128)S(1)} %copy-done.1, f32[512]{0:T(512)S(1)} %get-tuple-element.9), kind=kOutput, calls=%fused_computation.8 | convolution fusion | flops 2140467200 | bytes 5213184 | tf_op jit(solution)/shard_map/dot_general | solution.py:90
Async XLA Ops:
  6.5 1.1 copy-start
  6.5 127.2 %all-gather.2.cloned.1.call-start = ((), (), s32[]{:S(2)}) async-start(), calls=%async_computation.4 | async-start | bytes 9191424 | tf_op jit(solution)/shard_map/all_gather | solution.py:77
  74.7 85.1 %all-to-all-start.2 = ((f32[16,32,640]{2,1,0:T(8,128)}), f32[16,32,640]{2,1,0:T(8,128)S(1)}, u32[]{:S(2)}, u32[]{:S(2)}) async-start(f32[16,32,640]{2,1,0:T(8,128)} %broadcast_in_dim.4), calls=%async_computation.2 | async-start | bytes 2621440 | tf_op jit(solution)/shard_map/all_to_all | solution.py:19
  81.2 172.9 %all-reduce.2.cloned.1.call-start = ((), (), s32[]{:S(2)}) async-start(), calls=%async_computation.5 | async-start | bytes 4456448 | tf_op jit(solution)/shard_map/psum | solution.py:81
  155.7 0.7 copy-start.2
  254.0 4.5 %copy-start.1 = (f32[1024,544]{0,1:T(8,128)S(1)}, f32[1024,544]{0,1:T(8,128)}, u32[]{:S(2)}) copy-start(f32[1024,544]{0,1:T(8,128)} %all-reduce.2.cloned.1.call-done) | copy-start | bytes 6684676
Sparse Core Ops, SparseCore 0:
  9.2 124.5 all-gather.1
  155.9 98.0 all-reduce.1
where the time goes:
time: 276 us
  waiting for transfers between devices  141 us (51%)
  blocking collectives  66.2 us (24%)
  matrix products  41 us (15%)
  between operations  16.1 us (6%)
  starting transfers between devices  6.48 us (2%)
  local copies, waits for them, and re-layouts  2.9 us (1%)
    psum x1, waiting for transfers between devices, per_device(): rotated_acts = lax.psum(partial_acts, 'narrow')  87.8 us
    all_to_all x1, blocking collectives, summed_rows(): lax.all_to_all(nearer, far, split_axis=0, concat_axis=0, tiled=True)  54.5 us
    all_gather x1, waiting for transfers between devices, per_device(): gathered = lax.all_gather(activations, WIDE, axis=0, tiled=True)  52.6 us
    dot_general x1, matrix products, per_device(): jnp.dot(gathered, act_basis, precision=highest, preferred_element_type=jn...  21.9 us
    dot_general x4, matrix products, per_device(): jnp.dot(acts_window.T, grads_window, precision=highest, preferred_element...  15.1 us
    all_to_all x1, starting transfers between devices, from_everyone(): lax.all_to_all(jnp.broadcast_to(value[None], (devices, *value.shape)), ax...  6.44 us
    all_to_all x1, blocking collectives, from_everyone(): lax.all_to_all(jnp.broadcast_to(value[None], (devices, *value.shape)), ax...  5.84 us
    all_to_all x1, blocking collectives, sent_and_summed(): lax.all_to_all(blocks, axis, split_axis=0, concat_axis=0, tiled=True)  5.84 us
  transfers between devices with their start and end apart: 3, of which 2 were waited for; matrix products, arithmetic and copies ran while one was open for 11% of the time, Pallas kernels for 0%

commit v1 on v0

--- a/solution.py
+++ b/solution.py
@@ -3,10 +3,18 @@
 from jax import lax
 from jax.sharding import Mesh
 from jax.sharding import PartitionSpec as P
+from jax.lax import all_to_all, axis_size
 
 SEQS = 4
 SEQ_MOST = 512
 WIDE = ("wide_0", "wide_1", "wide_2")
+
+
+def work_table(s0):
+    tile_out = jnp.concatenate(
+        all_to_all(jnp.stack([s0 for _ in range(axis_size(WIDE))], axis=0), WIDE, 0, 0), axis=0
+    )
+    return tile_out
 
 
 def filled_up(lines, devices):
@@ -74,7 +82,7 @@
 
 def per_device(activations, act_basis, grads, grad_basis, seq_ids):
     highest = lax.Precision.HIGHEST
-    gathered = lax.all_gather(activations, WIDE, axis=0, tiled=True)
+    gathered = work_table(activations)
     partial_acts = jnp.dot(
         gathered, act_basis, precision=highest, preferred_element_type=jnp.float32
     )

time: 276 us -> 421 us (1.53)
  waiting for transfers between devices: 141 us -> 283 us
  blocking collectives: 66.2 us -> 54.4 us
  starting transfers between devices: 6.48 us -> 16.2 us
  local copies, waits for them, and re-layouts: 2.9 us -> 8.1 us
    all_to_all x0 -> x1, waiting for transfers between devices: none -> 194 us  [work_table(): all_to_all(jnp.stack([s0 for _ in range(axis_size(WIDE))], axis=0), WIDE,...]
    all_gather x1 -> x0, waiting for transfers between devices: 52.6 us -> none  [per_device(): gathered = lax.all_gather(activations, WIDE, axis=0, tiled=True)]
    all_to_all x1, blocking collectives: 54.5 us -> 42.7 us  [summed_rows(): lax.all_to_all(nearer, far, split_axis=0, concat_axis=0, tiled=True)]
    all_to_all x1, waiting for transfers between devices: 0.01 us -> 5.62 us  [from_everyone(): lax.all_to_all(jnp.broadcast_to(value[None], (devices, *value.shape)), ax...]
    all_to_all x1, starting transfers between devices: 6.44 us -> 11.4 us  [from_everyone(): lax.all_to_all(jnp.broadcast_to(value[None], (devices, *value.shape)), ax...]
    all_to_all x0 -> x1, starting transfers between devices: none -> 4.75 us  [work_table(): all_to_all(jnp.stack([s0 for _ in range(axis_size(WIDE))], axis=0), WIDE,...]
    another operation x0 -> x1, local copies, waits for them, and re-layouts: none -> 4.47 us  [work_table(): jnp.stack([s0 for _ in range(axis_size(WIDE))], axis=0)]
    psum x1, waiting for transfers between devices: 87.8 us -> 83.3 us  [per_device(): rotated_acts = lax.psum(partial_acts, 'narrow')]
  transfers between devices with their start and end apart: 3 -> 3, of which waited for: 2 -> 3; matrix products, arithmetic and copies ran while one was open for 11% -> 6% of each run, Pallas kernels for 0% -> 0%
where the time goes in v1:
time: 421 us
  waiting for transfers between devices  283 us (67%)
  blocking collectives  54.4 us (13%)
  matrix products  41 us (10%)
  starting transfers between devices  16.2 us (4%)
  between operations  16.1 us (4%)
  local copies, waits for them, and re-layouts  8.1 us (2%)
    all_to_all x1, waiting for transfers between devices, work_table(): all_to_all(jnp.stack([s0 for _ in range(axis_size(WIDE))], axis=0), WIDE,...  194 us
    psum x1, waiting for transfers between devices, per_device(): rotated_acts = lax.psum(partial_acts, 'narrow')  83.3 us
    all_to_all x1, blocking collectives, summed_rows(): lax.all_to_all(nearer, far, split_axis=0, concat_axis=0, tiled=True)  42.7 us
    dot_general x1, matrix products, per_device(): jnp.dot(gathered, act_basis, precision=highest, preferred_element_type=jn...  21.9 us
    dot_general x4, matrix products, per_device(): jnp.dot(acts_window.T, grads_window, precision=highest, preferred_element...  15.1 us
    all_to_all x1, starting transfers between devices, from_everyone(): lax.all_to_all(jnp.broadcast_to(value[None], (devices, *value.shape)), ax...  11.4 us
  transfers between devices with their start and end apart: 3, of which 3 were waited for; matrix products, arithmetic and copies ran while one was open for 6% of the time, Pallas kernels for 0%

profile of v1, /device:TPU:32, one launch (start us, length us, event | category | flops | bytes accessed | tf_op | source)
XLA Modules:
  0.0 420.9 jit_solution(15228253331422481288)
XLA Ops:
  6.5 0.0 copy-start
  6.5 1.1 copy-done
  7.6 3.9 fusion.29
  11.6 0.2 copy.11
  11.8 5.8 %all_to_all.25 = f32[2,16,32,640]{3,2,1,0:T(8,128)S(1)} all-to-all(f32[2,16,32,640]{3,2,1,0:T(8,128)S(1)} %bitcast.16), channel_id=1, replica_groups=mesh['wide_0'=2,'wide_1'=8,'wide_2'=2,'narrow'=8] {'wide_2'}, dimensions={0} | all-to-all | bytes 5242880 | tf_op jit(solution)/shard_map/all_to_all | solution.py:53
  17.6 1.3 reduce_sum.55
  18.9 0.0 copy-start.2
  18.9 42.7 %all_to_all.26 = f32[16,32,640]{2,1,0:T(8,128)S(1)} all-to-all(f32[16,32,640]{2,1,0:T(8,128)} %reduce_sum.55), channel_id=1, replica_groups=mesh['wide_0'=2,'wide_1'=8,'wide_2'=2,'narrow'=8] {'wide_0','wide_1'}, dimensions={0} | all-to-all | bytes 2621440 | tf_op jit(solution)/shard_map/all_to_all | solution.py:61
  61.7 0.0 copy-done.2
  61.7 4.5 %stack.2 = f32[32,32,2176]{2,1,0:T(8,128)} broadcast(f32[32,2176]{1,0:T(8,128)S(1)} %copy-done.2), dimensions={1,2} | broadcast | bytes 9191424 | tf_op jit(solution)/shard_map/stack | solution.py:15
  66.1 4.8 %all-to-all-start = ((f32[32,32,2176]{2,1,0:T(8,128)}), f32[32,32,2176]{2,1,0:T(8,128)}, u32[]{:S(2)}, u32[]{:S(2)}) async-start(f32[32,32,2176]{2,1,0:T(8,128)} %stack.2), calls=%async_computation | async-start | bytes 17825792 | tf_op jit(solution)/shard_map/all_to_all | solution.py:15
  70.9 0.1 reduce_sum.56
  71.0 194.0 %all-to-all-done = f32[32,32,2176]{2,1,0:T(8,128)} async-done(((f32[32,32,2176]{2,1,0:T(8,128)}), f32[32,32,2176]{2,1,0:T(8,128)}, u32[]{:S(2)}, u32[]{:S(2)}) %all-to-all-start) | async-done | bytes 8912928 | tf_op jit(solution)/shard_map/all_to_all | solution.py:15
  264.9 1.2 broadcast_in_dim.4
  266.1 11.4 %all-to-all-start.3 = ((f32[16,32,640]{2,1,0:T(8,128)}), f32[16,32,640]{2,1,0:T(8,128)S(1)}, u32[]{:S(2)}, u32[]{:S(2)}) async-start(f32[16,32,640]{2,1,0:T(8,128)} %broadcast_in_dim.4), calls=%async_computation.3 | async-start | bytes 2621440 | tf_op jit(solution)/shard_map/all_to_all | solution.py:27
  277.5 0.0 all-reduce.2.cloned.1.call-start
  277.5 21.9 %fusion.28 = f32[1024,544]{0,1:T(8,128)} fusion(f32[1024,2176]{1,0:T(8,128)} %bitcast, f32[2176,544]{0,1:T(8,128)} %param.6), kind=kOutput, calls=%fused_computation.41 | convolution fusion | flops 14545846272 | bytes 15876096 | tf_op jit(solution)/shard_map/dot_general | solution.py:86
  299.5 0.0 copy-start.3
  299.5 0.0 all-reduce.2.cloned.1.call-update
  299.5 0.7 copy-done.3
  300.2 0.7 convert_reduce_fusion
  303.5 0.1 fusion.27
  303.6 5.6 %all-to-all-done.3 = f32[16,32,640]{2,1,0:T(8,128)S(1)} async-done(((f32[16,32,640]{2,1,0:T(8,128)}), f32[16,32,640]{2,1,0:T(8,128)S(1)}, u32[]{:S(2)}, u32[]{:S(2)}) %all-to-all-start.3) | async-done | bytes 1310752 | tf_op jit(solution)/shard_map/all_to_all | solution.py:27
  309.2 0.3 broadcast_in_dim.5
  309.5 5.8 %all_to_all.27 = f32[2,16,32,640]{3,2,1,0:T(8,128)S(1)} all-to-all(f32[2,16,32,640]{3,2,1,0:T(8,128)S(1)} %broadcast_in_dim.5), channel_id=1, replica_groups=mesh['wide_0'=2,'wide_1'=8,'wide_2'=2,'narrow'=8] {'wide_2'}, dimensions={0} | all-to-all | bytes 5242880 | tf_op jit(solution)/shard_map/all_to_all | solution.py:27
  315.4 0.2 copy.9
  315.6 83.3 %all-reduce.2.cloned.1.call-done = f32[1024,544]{0,1:T(8,128)} async-done(((f32[1024,544]{0,1:T(8,128)}), f32[1024,544]{0,1:T(8,128)}) %all-reduce.2.cloned.1.call-update) | async-done | bytes 2228240 | tf_op jit(solution)/shard_map/psum | solution.py:89
  398.9 0.0 copy-start.1
  398.9 4.5 %convolution_multiply_fusion.1 = f32[544,640]{1,0:T(8,128)S(1)} fusion(f32[1024,640]{1,0:T(8,128)S(1)} %bitcast.12, s32[]{:T(128)S(6)} %select_n.10, f32[1024,544]{0,1:T(8,128)} %all-reduce.2.cloned.1.call-done, f32[512]{0:T(512)S(1)} %get-tuple-element.10), kind=kOutput, calls=%fused_computation.2 | convolution fusion | flops 2139770880 | bytes 3820544 | tf_op jit(solution)/shard_map/dot_general | solution.py:98
  403.4 0.0 copy-done.1
  403.4 3.1 convolution_multiply_fusion.2
  406.6 3.2 fusion.1
  409.8 4.2 %fusion.3 = f32[544,640]{1,0:T(8,128)} fusion(f32[544,640]{1,0:T(8,128)S(1)} %fusion.1, f32[1024,640]{1,0:T(8,128)S(1)} %bitcast.15, s32[]{:T(128)S(6)} %select_n.11, f32[1024,544]{0,1:T(8,128)S(1)} %copy-done.1, f32[512]{0:T(512)S(1)} %get-tuple-element.9), kind=kOutput, calls=%fused_computation.8 | convolution fusion | flops 2140467200 | bytes 5213184 | tf_op jit(solution)/shard_map/dot_general | solution.py:98
Async XLA Ops:
  6.5 1.1 copy-start
  18.9 42.7 %copy-start.2 = (f32[32,2176]{1,0:T(8,128)S(1)}, f32[32,2176]{1,0:T(8,128)}, u32[]{:S(2)}) copy-start(f32[32,2176]{1,0:T(8,128)} %param.5) | copy-start | bytes 835588
  66.1 198.8 %all-to-all-start = ((f32[32,32,2176]{2,1,0:T(8,128)}), f32[32,32,2176]{2,1,0:T(8,128)}, u32[]{:S(2)}, u32[]{:S(2)}) async-start(f32[32,32,2176]{2,1,0:T(8,128)} %stack.2), calls=%async_computation | async-start | bytes 17825792 | tf_op jit(solution)/shard_map/all_to_all | solution.py:15
  266.1 43.1 %all-to-all-start.3 = ((f32[16,32,640]{2,1,0:T(8,128)}), f32[16,32,640]{2,1,0:T(8,128)S(1)}, u32[]{:S(2)}, u32[]{:S(2)}) async-start(f32[16,32,640]{2,1,0:T(8,128)} %broadcast_in_dim.4), calls=%async_computation.3 | async-start | bytes 2621440 | tf_op jit(solution)/shard_map/all_to_all | solution.py:27
  277.5 121.4 %all-reduce.2.cloned.1.call-start = ((), (), s32[]{:S(2)}) async-start(), calls=%async_computation.5 | async-start | bytes 4456448 | tf_op jit(solution)/shard_map/psum | solution.py:89
  299.5 0.7 copy-start.3
  398.9 4.5 %copy-start.1 = (f32[1024,544]{0,1:T(8,128)S(1)}, f32[1024,544]{0,1:T(8,128)}, u32[]{:S(2)}) copy-start(f32[1024,544]{0,1:T(8,128)} %all-reduce.2.cloned.1.call-done) | copy-start | bytes 6684676
Sparse Core Ops, SparseCore 0:
  299.6 99.2 all-reduce.1
